TPU v7x, 32 devices: a whole 2x2x4 slice. The times are simulated.
32 devices in a mesh: row: 4 (over y, x), col: 8 (over z, core).
Axes of the slice: x: 2, y: 2, z: 4, core: 2. Of those that a mesh axis runs over, the one named last changes fastest.
Arguments:
- tiles: bfloat16 [256, 256, 256], P(('row', 'col')), may hold values from -0.09375 to 0.09375
- tile_rows: int32 [256], P(('row', 'col')), may hold values from 0 to 3, as said below
- tile_cols: int32 [256], P(('row', 'col')), may hold values from 0 to 1
- tile_count: int32 [32], P(('row', 'col')), may hold values from 0 to 8, as said below
- bounds: float32 [2], replicated, may hold values from -1 to 2, as said below
- vectors: float32 [4096, 128], P(('row', 'col')), may hold values from -6 to 6
Outputs:
- filtered: float32 [4096, 128], P(('row', 'col'))
- gram: float32 [128, 128], replicated
Inputs may be any that keep to these rules, and one draw needn't show every extreme that they name: `tile_rows`: within each device the first tile_count slots name distinct blocks with global block row I <= global block column J; the device's diagonal blocks (I = J) come first; every diagonal block of the Hamiltonian is stored; slots after the live ones hold valid indices but are not part of the matrix. `tile_count`: devices whose block rows all lie below their block columns have no live slot; some device has all 8 slots live. bounds[0] < -0.5 and bounds[1] > 1.0.
All inputs are finite; a program needn't handle non-finite values.
Results may differ from a plain program's by a relative error of at most 0.0037.
Values may be sent and summed in bfloat16 or wider, within the bound.
A program may use at most 64 MiB of HBM per device.

v0:
```python
import jax
import jax.numpy as jnp
from jax import lax
from jax.sharding import PartitionSpec as P

BLK_COL = 2


def spread(block, axis, holder):
    block = jnp.where(lax.axis_index(axis) == holder, block, jnp.zeros_like(block))
    return lax.psum(block, axis)


def on_device(tiles, tile_rows, tile_cols, tile_count, bounds, vectors):
    col_ratio = lax.axis_size("col") // lax.axis_size("row")
    col_index = lax.axis_index("col")
    row_index = lax.axis_index("row")
    root_row = col_index // col_ratio
    slot_total = tiles.shape[0]
    block_size = tiles.shape[1]
    share_rows = vectors.shape[0]
    width_vecs = vectors.shape[1]
    group_rows = share_rows * lax.axis_size("col")
    group_blocks = group_rows // block_size
    column_rows = BLK_COL * block_size
    total_rows = share_rows * lax.axis_size("row") * lax.axis_size("col")
    offset = col_index % col_ratio * column_rows
    live_mask = (jnp.arange(slot_total, dtype=jnp.int32) < tile_count[0]).astype(jnp.bfloat16)
    owner_flag = (row_index == root_row).astype(jnp.float32)
    center = (bounds[1] + bounds[0]) * 0.5
    halfwidth = (bounds[1] - bounds[0]) * 0.5

    def apply_hamiltonian(current_vec):
        vector_panel = current_vec.astype(jnp.bfloat16)
        row_panel = lax.all_gather(vector_panel, "col", axis=0, tiled=True)
        col_piece = lax.dynamic_slice_in_dim(row_panel, offset, column_rows, 0)
        col_panel = spread(col_piece, "row", root_row)
        row_input = row_panel.reshape(group_blocks, block_size, width_vecs)
        col_input = col_panel.reshape(BLK_COL, block_size, width_vecs)
        start_rows = jnp.zeros((group_blocks, block_size, width_vecs), jnp.float32)
        start_cols = jnp.zeros((BLK_COL, block_size, width_vecs), jnp.float32)
        masked_cols = col_input[tile_cols] * live_mask[:, None, None]
        masked_rows = row_input[tile_rows] * live_mask[:, None, None]
        forward = jnp.einsum("tab,tbk->tak", tiles, masked_cols, preferred_element_type=jnp.float32)
        backward = jnp.einsum(
            "tab,tak->tbk", tiles, masked_rows, preferred_element_type=jnp.float32
        )
        row_part = start_rows.at[tile_rows].add(forward)
        col_part = start_cols.at[tile_cols].add(backward)
        column_total = lax.psum(col_part, "row")
        row_part = row_part.reshape(group_rows, width_vecs)
        present = lax.dynamic_slice_in_dim(row_part, offset, column_rows, 0)
        updated = present + owner_flag * column_total.reshape(column_rows, width_vecs)
        row_part = lax.dynamic_update_slice_in_dim(row_part, updated, offset, 0)
        return lax.psum_scatter(row_part, "col", scatter_dimension=0, tiled=True)

    current_vec = (apply_hamiltonian(vectors) - center * vectors) / halfwidth
    image = apply_hamiltonian(current_vec)
    following = 2.0 * (image - center * current_vec) / halfwidth - vectors
    current_vec = following
    gram_local = lax.dot_general(
        current_vec,
        current_vec,
        (((0,), (0,)), ((), ())),
        precision=lax.Precision.HIGHEST,
        preferred_element_type=jnp.float32,
    )
    gram_total = lax.psum(gram_local, ("row", "col"))
    return (current_vec, gram_total / total_rows)


def solution(mesh):
    in_specs = (
        P(("row", "col"), None, None),
        P(("row", "col")),
        P(("row", "col")),
        P(("row", "col")),
        P(),
        P(("row", "col"), None),
    )
    out_specs = (P(("row", "col"), None), P())
    return jax.shard_map(
        on_device, mesh=mesh, in_specs=in_specs, out_specs=out_specs, check_vma=False
    )
```

profile of v0, /device:TPU:1, one launch (start us, length us, event | category | flops | bytes accessed | tf_op | source)
XLA Modules:
  0.0 414.4 jit_solution(1064199134010569408)
XLA Ops:
  7.2 0.9 convert_element_type.16
  8.2 15.8 %all_gather.6 = bf16[1024,128]{1,0:T(8,128)(2,1)S(1)} all-gather(bf16[128,128]{1,0:T(8,128)(2,1)S(1)} %convert_element_type.16), channel_id=1, replica_groups=mesh['row'=4,'col'=8] {'col'}, dimensions={0}, use_global_device_ids=true | all-gather | bytes 294912 | tf_op jit(solution)/shard_map/all_gather | solution.py:35
  27.8 1.3 scatter_fusion.1
  29.9 37.0 %all-reduce.6.cloned.1.call-done = bf16[2,256,128]{2,1,0:T(8,128)(2,1)} async-done(((bf16[2,256,128]{2,1,0:T(8,128)(2,1)}), bf16[2,256,128]{2,1,0:T(8,128)(2,1)}) %all-reduce.6.cloned.1.call-update) | async-done | bytes 131088 | tf_op jit(solution)/shard_map/psum | solution.py:11
  66.9 1.5 gather_fusion
  68.5 1.7 convolution_bitcast_fusion.3
  70.2 1.5 copy.13
  71.8 1.3 scatter_fusion
  73.1 39.9 %all-reduce.8.cloned.1.call-done = f32[2,256,128]{2,1,0:T(8,128)} async-done(((f32[2,256,128]{2,1,0:T(8,128)}), f32[2,256,128]{2,1,0:T(8,128)}) %all-reduce.8.cloned.1.call-update) | async-done | bytes 262160 | tf_op jit(solution)/shard_map/psum | solution.py:50
  113.1 1.0 broadcast_multiply_fusion.1
  118.1 25.2 %reduce-scatter.3.cloned.1.call-done = f32[128,128]{1,0:T(8,128)} async-done(((f32[1024,128]{1,0:T(8,128)}), f32[128,128]{1,0:T(8,128)}) %reduce-scatter.3.cloned.1.call-update) | async-done | bytes 65552 | tf_op jit(solution)/shard_map/reduce_scatter | solution.py:55
  144.2 18.0 %all_gather.7 = bf16[1024,128]{1,0:T(8,128)(2,1)S(1)} all-gather(bf16[128,128]{1,0:T(8,128)(2,1)S(1)} %fusion.8), channel_id=1, replica_groups=mesh['row'=4,'col'=8] {'col'}, dimensions={0}, use_global_device_ids=true | all-gather | bytes 294912 | tf_op jit(solution)/shard_map/all_gather | solution.py:35
  164.4 1.3 scatter_fusion.3
  166.6 36.5 %all-reduce.10.cloned.1.call-done = bf16[2,256,128]{2,1,0:T(8,128)(2,1)} async-done(((bf16[2,256,128]{2,1,0:T(8,128)(2,1)}), bf16[2,256,128]{2,1,0:T(8,128)(2,1)}) %all-reduce.10.cloned.1.call-update) | async-done | bytes 131088 | tf_op jit(solution)/shard_map/psum | solution.py:11
  203.1 1.5 gather_fusion.2
  204.7 1.7 convolution_bitcast_fusion.1
  206.4 1.5 copy.17
  208.0 1.3 scatter_fusion.2
  209.3 39.5 %all-reduce.12.cloned.1.call-done = f32[2,256,128]{2,1,0:T(8,128)} async-done(((f32[2,256,128]{2,1,0:T(8,128)}), f32[2,256,128]{2,1,0:T(8,128)}) %all-reduce.12.cloned.1.call-update) | async-done | bytes 262160 | tf_op jit(solution)/shard_map/psum | solution.py:50
  248.8 1.0 broadcast_multiply_fusion
  250.7 28.2 %reduce-scatter.5.cloned.1.call-done = f32[128,128]{1,0:T(8,128)} async-done(((f32[1024,128]{1,0:T(8,128)}), f32[128,128]{1,0:T(8,128)}) %reduce-scatter.5.cloned.1.call-update) | async-done | bytes 65552 | tf_op jit(solution)/shard_map/reduce_scatter | solution.py:55
  279.8 0.9 fusion.10
  280.8 125.3 %all-reduce.14.cloned.1.call-done = f32[128,128]{1,0:T(8,128)} async-done(((f32[128,128]{1,0:T(8,128)}), f32[128,128]{1,0:T(8,128)}) %all-reduce.14.cloned.1.call-update) | async-done | bytes 65552 | tf_op jit(solution)/shard_map/psum | solution.py:68
  406.1 1.5 broadcast_multiply_fusion.2
  (58 shorter events, 11.0 us)
Async XLA Ops:
  7.2 19.5 %copy-start = (bf16[8,256,256]{2,1,0:T(8,128)(2,1)S(1)}, bf16[8,256,256]{2,1,0:T(8,128)(2,1)}, u32[]{:S(2)}) copy-start(bf16[8,256,256]{2,1,0:T(8,128)(2,1)} %param.6) | copy-start | bytes 3145732
  7.2 59.8 %all-reduce.6.cloned.1.call-start = ((), (), s32[]{:S(2)}) async-start(), calls=%async_computation.2 | async-start | bytes 262144 | tf_op jit(solution)/shard_map/psum | solution.py:11
  24.6 88.4 %all-reduce.8.cloned.1.call-start = ((), (), s32[]{:S(2)}) async-start(), calls=%async_computation.3 | async-start | bytes 524288 | tf_op jit(solution)/shard_map/psum | solution.py:50
  25.3 0.7 copy-start.9
  27.1 0.7 copy-start.10
  29.1 0.7 copy-start.4
  29.8 113.5 %reduce-scatter.3.cloned.1.call-start = ((), (), s32[]{:S(2)}) async-start(), calls=%async_computation.4 | async-start | bytes 589824 | tf_op jit(solution)/shard_map/reduce_scatter | solution.py:55
  114.1 0.8 copy-start.2
  114.1 0.9 copy-start.8
  114.1 29.3 %copy-start.5 = (f32[128,128]{1,0:T(8,128)S(1)}, f32[128,128]{1,0:T(8,128)}, u32[]{:S(2)}) copy-start(f32[128,128]{1,0:T(8,128)} %param.11) | copy-start | bytes 196612
  114.9 88.2 %all-reduce.10.cloned.1.call-start = ((), (), s32[]{:S(2)}) async-start(), calls=%async_computation.5 | async-start | bytes 262144 | tf_op jit(solution)/shard_map/psum | solution.py:11
  163.6 85.2 %all-reduce.12.cloned.1.call-start = ((), (), s32[]{:S(2)}) async-start(), calls=%async_computation.6 | async-start | bytes 524288 | tf_op jit(solution)/shard_map/psum | solution.py:50
  165.8 0.7 copy-start.3
  166.5 112.4 %reduce-scatter.5.cloned.1.call-start = ((), (), s32[]{:S(2)}) async-start(), calls=%async_computation.7 | async-start | bytes 589824 | tf_op jit(solution)/shard_map/reduce_scatter | solution.py:55
  249.9 0.8 copy-start.1
  249.9 29.1 %copy-start.7 = (f32[128,128]{1,0:T(8,128)S(1)}, f32[128,128]{1,0:T(8,128)}, u32[]{:S(2)}) copy-start(f32[128,128]{1,0:T(8,128)} %reduce-scatter.3.cloned.1.call-done) | copy-start | bytes 196612
  250.7 155.4 %all-reduce.14.cloned.1.call-start = ((), (), s32[]{:S(2)}) async-start(), calls=%async_computation.8 | async-start | bytes 131072 | tf_op jit(solution)/shard_map/psum | solution.py:68
  279.8 0.9 copy-start.6
Sparse Core Ops, SparseCore 0:
  24.8 42.1 all-reduce.5
  70.1 42.8 all-reduce.7
  115.3 28.0 reduce-scatter.2
  163.7 39.3 all-reduce.9
  205.9 42.9 all-reduce.11
  251.0 27.8 reduce-scatter.4
  285.1 120.9 all-reduce.13
where the time goes:
time: 415 us; the launch traced here: 414 us
  waiting for transfers between devices  332 us (80%)
  blocking collectives  33.8 us (8%)
  between operations  17.7 us (4%)
  local copies, waits for them, and re-layouts  12.8 us (3%)
  other arithmetic  12.8 us (3%)
  matrix products  5.15 us (1%)
    psum x1, waiting for transfers between devices, on_device(): gram_total = lax.psum(gram_local, ('row', 'col'))  125 us
    psum x2, waiting for transfers between devices, apply_hamiltonian(): column_total = lax.psum(col_part, 'row')  79.5 us
    psum x2, waiting for transfers between devices, spread(): return lax.psum(block, axis)  73.6 us
    reduce_scatter x2, waiting for transfers between devices, apply_hamiltonian(): return lax.psum_scatter(row_part, 'col', scatter_dimension=0, tiled=True)  53.5 us
    all_gather x2, blocking collectives, apply_hamiltonian(): row_panel = lax.all_gather(vector_panel, 'col', axis=0, tiled=True)  33.8 us
  transfers between devices with their start and end apart: 7, of which 7 were waited for; matrix products, arithmetic and copies ran while one was open for 4% of the time, Pallas kernels for 0%

commit v1 on v0

--- a/solution.py
+++ b/solution.py
@@ -32,7 +32,14 @@
 
     def apply_hamiltonian(current_vec):
         vector_panel = current_vec.astype(jnp.bfloat16)
-        row_panel = lax.all_gather(vector_panel, "col", axis=0, tiled=True)
+        ring = [vector_panel]
+        for hop in range(7):
+            ring.append(lax.ppermute(ring[-1], "col", [(dev, (dev + 1) % 8) for dev in range(8)]))
+        row_panel = jnp.roll(
+            jnp.concatenate(ring[::-1], axis=0),
+            (lax.axis_index("col") + 1) * ring[0].shape[0],
+            axis=0,
+        )
         col_piece = lax.dynamic_slice_in_dim(row_panel, offset, column_rows, 0)
         col_panel = spread(col_piece, "row", root_row)
         row_input = row_panel.reshape(group_blocks, block_size, width_vecs)

time: 415 us -> 459 us (1.11)
  waiting for transfers between devices: 332 us -> 397 us
  blocking collectives: 33.8 us -> 0 us
  starting transfers between devices: 0.29 us -> 10 us
    ppermute x0 -> x14, waiting for transfers between devices: none -> 57.7 us  [apply_hamiltonian(): lax.ppermute(ring[-1], 'col', [(dev, (dev + 1) % 8) for dev in range(8)])]
    all_gather x2 -> x0, blocking collectives: 33.8 us -> none  [apply_hamiltonian(): row_panel = lax.all_gather(vector_panel, 'col', axis=0, tiled=True)]
    ppermute x0 -> x14, starting transfers between devices: none -> 9.71 us  [apply_hamiltonian(): lax.ppermute(ring[-1], 'col', [(dev, (dev + 1) % 8) for dev in range(8)])]
    psum x2, waiting for transfers between devices: 73.6 us -> 81.4 us  [spread(): return lax.psum(block, axis)]
  transfers between devices with their start and end apart: 7 -> 21, of which waited for: 7 -> 21; matrix products, arithmetic and copies ran while one was open for 4% -> 4% of each run, Pallas kernels for 0% -> 0%
where the time goes in v1:
time: 459 us
  waiting for transfers between devices  397 us (86%)
  between operations  17.7 us (4%)
  other arithmetic  15.6 us (3%)
  local copies, waits for them, and re-layouts  12.8 us (3%)
  starting transfers between devices  10 us (2%)
  matrix products  5.15 us (1%)
    psum x1, waiting for transfers between devices, on_device(): gram_total = lax.psum(gram_local, ('row', 'col'))  125 us
    psum x2, waiting for transfers between devices, spread(): return lax.psum(block, axis)  81.4 us
    psum x2, waiting for transfers between devices, apply_hamiltonian(): column_total = lax.psum(col_part, 'row')  79.5 us
    ppermute x14, waiting for transfers between devices, apply_hamiltonian(): lax.ppermute(ring[-1], 'col', [(dev, (dev + 1) % 8) for dev in range(8)])  57.7 us
    reduce_scatter x2, waiting for transfers between devices, apply_hamiltonian(): return lax.psum_scatter(row_part, 'col', scatter_dimension=0, tiled=True)  53.5 us
    ppermute x14, starting transfers between devices, apply_hamiltonian(): lax.ppermute(ring[-1], 'col', [(dev, (dev + 1) % 8) for dev in range(8)])  9.71 us
  transfers between devices with their start and end apart: 21, of which 21 were waited for; matrix products, arithmetic and copies ran while one was open for 4% of the time, Pallas kernels for 0%

profile of v1, /device:TPU:1, one launch (start us, length us, event | category | flops | bytes accessed | tf_op | source)
XLA Modules:
  0.0 458.7 jit_solution(7723361995786857978)
XLA Ops:
  8.2 2.7 collective-permute-start
  11.9 2.3 collective-permute-start.1
  15.2 2.3 collective-permute-start.2
  17.5 2.6 collective-permute-done.2
  20.9 4.4 collective-permute-done.3
  25.3 5.1 %collective-permute-done.4 = bf16[128,128]{1,0:T(8,128)(2,1)S(1)} collective-permute-done((bf16[128,128]{1,0:T(8,128)(2,1)S(1)}, bf16[128,128]{1,0:T(8,128)(2,1)S(1)}, u32[]{:S(2)}, u32[]{:S(2)}) %collective-permute-start.4) | collective-permute-done | bytes 32800 | tf_op jit(solution)/shard_map/ppermute | solution.py:37
  31.1 4.5 collective-permute-done.5
  35.6 5.1 %collective-permute-done.6 = bf16[128,128]{1,0:T(8,128)(2,1)S(1)} collective-permute-done((bf16[128,128]{1,0:T(8,128)(2,1)S(1)}, bf16[128,128]{1,0:T(8,128)(2,1)S(1)}, u32[]{:S(2)}, u32[]{:S(2)}) %collective-permute-start.6) | collective-permute-done | bytes 32800 | tf_op jit(solution)/shard_map/ppermute | solution.py:37
  47.3 40.6 %all-reduce.6.cloned.1.call-done = bf16[2,256,128]{2,1,0:T(8,128)(2,1)} async-done(((bf16[2,256,128]{2,1,0:T(8,128)(2,1)}), bf16[2,256,128]{2,1,0:T(8,128)(2,1)}) %all-reduce.6.cloned.1.call-update) | async-done | bytes 131088 | tf_op jit(solution)/shard_map/psum | solution.py:11
  89.5 1.7 convolution_bitcast_fusion.3
  94.1 39.9 %all-reduce.8.cloned.1.call-done = f32[2,256,128]{2,1,0:T(8,128)} async-done(((f32[2,256,128]{2,1,0:T(8,128)}), f32[2,256,128]{2,1,0:T(8,128)}) %all-reduce.8.cloned.1.call-update) | async-done | bytes 262160 | tf_op jit(solution)/shard_map/psum | solution.py:57
  139.1 25.2 %reduce-scatter.3.cloned.1.call-done = f32[128,128]{1,0:T(8,128)} async-done(((f32[1024,128]{1,0:T(8,128)}), f32[128,128]{1,0:T(8,128)}) %reduce-scatter.3.cloned.1.call-update) | async-done | bytes 65552 | tf_op jit(solution)/shard_map/reduce_scatter | solution.py:62
  166.8 3.2 collective-permute-done.7
  170.1 5.0 %collective-permute-done.8 = bf16[128,128]{1,0:T(8,128)(2,1)S(1)} collective-permute-done((bf16[128,128]{1,0:T(8,128)(2,1)S(1)}, bf16[128,128]{1,0:T(8,128)(2,1)S(1)}, u32[]{:S(2)}, u32[]{:S(2)}) %collective-permute-start.8) | collective-permute-done | bytes 32800 | tf_op jit(solution)/shard_map/ppermute | solution.py:37
  175.1 5.1 %collective-permute-done.9 = bf16[128,128]{1,0:T(8,128)(2,1)S(1)} collective-permute-done((bf16[128,128]{1,0:T(8,128)(2,1)S(1)}, bf16[128,128]{1,0:T(8,128)(2,1)S(1)}, u32[]{:S(2)}, u32[]{:S(2)}) %collective-permute-start.9) | collective-permute-done | bytes 32800 | tf_op jit(solution)/shard_map/ppermute | solution.py:37
  180.3 5.1 %collective-permute-done.10 = bf16[128,128]{1,0:T(8,128)(2,1)S(1)} collective-permute-done((bf16[128,128]{1,0:T(8,128)(2,1)S(1)}, bf16[128,128]{1,0:T(8,128)(2,1)S(1)}, u32[]{:S(2)}, u32[]{:S(2)}) %collective-permute-start.10) | collective-permute-done | bytes 32800 | tf_op jit(solution)/shard_map/ppermute | solution.py:37
  185.4 5.1 %collective-permute-done.11 = bf16[128,128]{1,0:T(8,128)(2,1)S(1)} collective-permute-done((bf16[128,128]{1,0:T(8,128)(2,1)S(1)}, bf16[128,128]{1,0:T(8,128)(2,1)S(1)}, u32[]{:S(2)}, u32[]{:S(2)}) %collective-permute-start.11) | collective-permute-done | bytes 32800 | tf_op jit(solution)/shard_map/ppermute | solution.py:37
  190.6 5.1 %collective-permute-done.12 = bf16[128,128]{1,0:T(8,128)(2,1)S(1)} collective-permute-done((bf16[128,128]{1,0:T(8,128)(2,1)S(1)}, bf16[128,128]{1,0:T(8,128)(2,1)S(1)}, u32[]{:S(2)}, u32[]{:S(2)}) %collective-permute-start.12) | collective-permute-done | bytes 32800 | tf_op jit(solution)/shard_map/ppermute | solution.py:37
  195.7 5.1 %collective-permute-done.13 = bf16[128,128]{1,0:T(8,128)(2,1)S(1)} collective-permute-done((bf16[128,128]{1,0:T(8,128)(2,1)S(1)}, bf16[128,128]{1,0:T(8,128)(2,1)S(1)}, u32[]{:S(2)}, u32[]{:S(2)}) %collective-permute-start.13) | collective-permute-done | bytes 32800 | tf_op jit(solution)/shard_map/ppermute | solution.py:37
  206.6 40.8 %all-reduce.10.cloned.1.call-done = bf16[2,256,128]{2,1,0:T(8,128)(2,1)} async-done(((bf16[2,256,128]{2,1,0:T(8,128)(2,1)}), bf16[2,256,128]{2,1,0:T(8,128)(2,1)}) %all-reduce.10.cloned.1.call-update) | async-done | bytes 131088 | tf_op jit(solution)/shard_map/psum | solution.py:11
  249.0 1.7 convolution_bitcast_fusion.1
  253.6 39.5 %all-reduce.12.cloned.1.call-done = f32[2,256,128]{2,1,0:T(8,128)} async-done(((f32[2,256,128]{2,1,0:T(8,128)}), f32[2,256,128]{2,1,0:T(8,128)}) %all-reduce.12.cloned.1.call-update) | async-done | bytes 262160 | tf_op jit(solution)/shard_map/psum | solution.py:57
  295.0 28.2 %reduce-scatter.5.cloned.1.call-done = f32[128,128]{1,0:T(8,128)} async-done(((f32[1024,128]{1,0:T(8,128)}), f32[128,128]{1,0:T(8,128)}) %reduce-scatter.5.cloned.1.call-update) | async-done | bytes 65552 | tf_op jit(solution)/shard_map/reduce_scatter | solution.py:62
  325.1 125.3 %all-reduce.14.cloned.1.call-done = f32[128,128]{1,0:T(8,128)} async-done(((f32[128,128]{1,0:T(8,128)}), f32[128,128]{1,0:T(8,128)}) %all-reduce.14.cloned.1.call-update) | async-done | bytes 65552 | tf_op jit(solution)/shard_map/psum | solution.py:75
  (102 shorter events, 35.0 us)
Async XLA Ops:
  7.2 37.3 %copy-start = (bf16[8,256,256]{2,1,0:T(8,128)(2,1)S(1)}, bf16[8,256,256]{2,1,0:T(8,128)(2,1)}, u32[]{:S(2)}) copy-start(bf16[8,256,256]{2,1,0:T(8,128)(2,1)} %param.8) | copy-start | bytes 3145732
  7.2 80.8 %all-reduce.6.cloned.1.call-start = ((), (), s32[]{:S(2)}) async-start(), calls=%async_computation.2 | async-start | bytes 262144 | tf_op jit(solution)/shard_map/psum | solution.py:11
  8.2 12.7 %copy-start.10 = (s32[8]{0:T(128)S(1)}, s32[8]{0:T(128)}, u32[]{:S(2)}) copy-start(s32[8]{0:T(128)} %param.10) | copy-start | bytes 100
  8.2 3.7 collective-permute-start
  11.9 3.3 collective-permute-start.1
  15.2 4.9 %collective-permute-start.2 = (bf16[128,128]{1,0:T(8,128)(2,1)S(1)}, bf16[128,128]{1,0:T(8,128)(2,1)S(1)}, u32[]{:S(2)}, u32[]{:S(2)}) collective-permute-start(bf16[128,128]{1,0:T(8,128)(2,1)S(1)} %collective-permute-done.1), channel_id=1, source_target_pairs={{0,1},{1,2},{2,3},{3,4},{4,5},{5,6},{6,7},{7,0},{8,9},{9,10},{10,1... | collective-permute-start | bytes 98312 | tf_op jit(solution)/shard_map/ppermute | solution.py:37
  20.1 5.1 %collective-permute-start.3 = (bf16[128,128]{1,0:T(8,128)(2,1)S(1)}, bf16[128,128]{1,0:T(8,128)(2,1)S(1)}, u32[]{:S(2)}, u32[]{:S(2)}) collective-permute-start(bf16[128,128]{1,0:T(8,128)(2,1)S(1)} %collective-permute-done.2), channel_id=1, source_target_pairs={{0,1},{1,2},{2,3},{3,4},{4,5},{5,6},{6,7},{7,0},{8,9},{9,10},{10,1... | collective-permute-start | bytes 98312 | tf_op jit(solution)/shard_map/ppermute | solution.py:37
  25.3 5.1 %collective-permute-start.4 = (bf16[128,128]{1,0:T(8,128)(2,1)S(1)}, bf16[128,128]{1,0:T(8,128)(2,1)S(1)}, u32[]{:S(2)}, u32[]{:S(2)}) collective-permute-start(bf16[128,128]{1,0:T(8,128)(2,1)S(1)} %collective-permute-done.3), channel_id=1, source_target_pairs={{0,1},{1,2},{2,3},{3,4},{4,5},{5,6},{6,7},{7,0},{8,9},{9,10},{10,1... | collective-permute-start | bytes 98312 | tf_op jit(solution)/shard_map/ppermute | solution.py:37
  30.4 5.1 %collective-permute-start.5 = (bf16[128,128]{1,0:T(8,128)(2,1)S(1)}, bf16[128,128]{1,0:T(8,128)(2,1)S(1)}, u32[]{:S(2)}, u32[]{:S(2)}) collective-permute-start(bf16[128,128]{1,0:T(8,128)(2,1)S(1)} %collective-permute-done.4), channel_id=1, source_target_pairs={{0,1},{1,2},{2,3},{3,4},{4,5},{5,6},{6,7},{7,0},{8,9},{9,10},{10,1... | collective-permute-start | bytes 98312 | tf_op jit(solution)/shard_map/ppermute | solution.py:37
  35.6 5.1 %collective-permute-start.6 = (bf16[128,128]{1,0:T(8,128)(2,1)S(1)}, bf16[128,128]{1,0:T(8,128)(2,1)S(1)}, u32[]{:S(2)}, u32[]{:S(2)}) collective-permute-start(bf16[128,128]{1,0:T(8,128)(2,1)S(1)} %collective-permute-done.5), channel_id=1, source_target_pairs={{0,1},{1,2},{2,3},{3,4},{4,5},{5,6},{6,7},{7,0},{8,9},{9,10},{10,1... | collective-permute-start | bytes 98312 | tf_op jit(solution)/shard_map/ppermute | solution.py:37
  43.7 90.3 %all-reduce.8.cloned.1.call-start = ((), (), s32[]{:S(2)}) async-start(), calls=%async_computation.3 | async-start | bytes 524288 | tf_op jit(solution)/shard_map/psum | solution.py:57
  47.3 117.1 %reduce-scatter.3.cloned.1.call-start = ((), (), s32[]{:S(2)}) async-start(), calls=%async_computation.4 | async-start | bytes 589824 | tf_op jit(solution)/shard_map/reduce_scatter | solution.py:62
  135.9 111.5 %all-reduce.10.cloned.1.call-start = ((), (), s32[]{:S(2)}) async-start(), calls=%async_computation.5 | async-start | bytes 262144 | tf_op jit(solution)/shard_map/psum | solution.py:11
  165.2 4.8 %collective-permute-start.7 = (bf16[128,128]{1,0:T(8,128)(2,1)S(1)}, bf16[128,128]{1,0:T(8,128)(2,1)S(1)}, u32[]{:S(2)}, u32[]{:S(2)}) collective-permute-start(bf16[128,128]{1,0:T(8,128)(2,1)S(1)} %fusion.14), channel_id=1, source_target_pairs={{0,1},{1,2},{2,3},{3,4},{4,5},{5,6},{6,7},{7,0},{8,9},{9,10},{10,1... | collective-permute-start | bytes 98312 | tf_op jit(solution)/shard_map/ppermute | solution.py:37
  170.0 5.1 %collective-permute-start.8 = (bf16[128,128]{1,0:T(8,128)(2,1)S(1)}, bf16[128,128]{1,0:T(8,128)(2,1)S(1)}, u32[]{:S(2)}, u32[]{:S(2)}) collective-permute-start(bf16[128,128]{1,0:T(8,128)(2,1)S(1)} %collective-permute-done.7), channel_id=1, source_target_pairs={{0,1},{1,2},{2,3},{3,4},{4,5},{5,6},{6,7},{7,0},{8,9},{9,10},{10,1... | collective-permute-start | bytes 98312 | tf_op jit(solution)/shard_map/ppermute | solution.py:37
  175.1 5.1 %collective-permute-start.9 = (bf16[128,128]{1,0:T(8,128)(2,1)S(1)}, bf16[128,128]{1,0:T(8,128)(2,1)S(1)}, u32[]{:S(2)}, u32[]{:S(2)}) collective-permute-start(bf16[128,128]{1,0:T(8,128)(2,1)S(1)} %collective-permute-done.8), channel_id=1, source_target_pairs={{0,1},{1,2},{2,3},{3,4},{4,5},{5,6},{6,7},{7,0},{8,9},{9,10},{10,1... | collective-permute-start | bytes 98312 | tf_op jit(solution)/shard_map/ppermute | solution.py:37
  180.3 5.1 %collective-permute-start.10 = (bf16[128,128]{1,0:T(8,128)(2,1)S(1)}, bf16[128,128]{1,0:T(8,128)(2,1)S(1)}, u32[]{:S(2)}, u32[]{:S(2)}) collective-permute-start(bf16[128,128]{1,0:T(8,128)(2,1)S(1)} %collective-permute-done.9), channel_id=1, source_target_pairs={{0,1},{1,2},{2,3},{3,4},{4,5},{5,6},{6,7},{7,0},{8,9},{9,10},{10,1... | collective-permute-start | bytes 98312 | tf_op jit(solution)/shard_map/ppermute | solution.py:37
  185.4 5.1 %collective-permute-start.11 = (bf16[128,128]{1,0:T(8,128)(2,1)S(1)}, bf16[128,128]{1,0:T(8,128)(2,1)S(1)}, u32[]{:S(2)}, u32[]{:S(2)}) collective-permute-start(bf16[128,128]{1,0:T(8,128)(2,1)S(1)} %collective-permute-done.10), channel_id=1, source_target_pairs={{0,1},{1,2},{2,3},{3,4},{4,5},{5,6},{6,7},{7,0},{8,9},{9,10},{10,1... | collective-permute-start | bytes 98312 | tf_op jit(solution)/shard_map/ppermute | solution.py:37
  190.6 5.1 %collective-permute-start.12 = (bf16[128,128]{1,0:T(8,128)(2,1)S(1)}, bf16[128,128]{1,0:T(8,128)(2,1)S(1)}, u32[]{:S(2)}, u32[]{:S(2)}) collective-permute-start(bf16[128,128]{1,0:T(8,128)(2,1)S(1)} %collective-permute-done.11), channel_id=1, source_target_pairs={{0,1},{1,2},{2,3},{3,4},{4,5},{5,6},{6,7},{7,0},{8,9},{9,10},{10,1... | collective-permute-start | bytes 98312 | tf_op jit(solution)/shard_map/ppermute | solution.py:37
  195.7 5.1 %collective-permute-start.13 = (bf16[128,128]{1,0:T(8,128)(2,1)S(1)}, bf16[128,128]{1,0:T(8,128)(2,1)S(1)}, u32[]{:S(2)}, u32[]{:S(2)}) collective-permute-start(bf16[128,128]{1,0:T(8,128)(2,1)S(1)} %collective-permute-done.12), channel_id=1, source_target_pairs={{0,1},{1,2},{2,3},{3,4},{4,5},{5,6},{6,7},{7,0},{8,9},{9,10},{10,1... | collective-permute-start | bytes 98312 | tf_op jit(solution)/shard_map/ppermute | solution.py:37
  203.7 89.4 %all-reduce.12.cloned.1.call-start = ((), (), s32[]{:S(2)}) async-start(), calls=%async_computation.6 | async-start | bytes 524288 | tf_op jit(solution)/shard_map/psum | solution.py:57
  206.6 116.6 %reduce-scatter.5.cloned.1.call-start = ((), (), s32[]{:S(2)}) async-start(), calls=%async_computation.7 | async-start | bytes 589824 | tf_op jit(solution)/shard_map/reduce_scatter | solution.py:62
  294.2 29.1 %copy-start.7 = (f32[128,128]{1,0:T(8,128)S(1)}, f32[128,128]{1,0:T(8,128)}, u32[]{:S(2)}) copy-start(f32[128,128]{1,0:T(8,128)} %reduce-scatter.3.cloned.1.call-done) | copy-start | bytes 196612
  295.0 155.4 %all-reduce.14.cloned.1.call-start = ((), (), s32[]{:S(2)}) async-start(), calls=%async_computation.8 | async-start | bytes 131072 | tf_op jit(solution)/shard_map/psum | solution.py:75
  (8 other events, 16.0 us)
Sparse Core Ops, SparseCore 0:
  43.8 44.0 all-reduce.5
  91.1 42.8 all-reduce.7
  136.3 28.0 reduce-scatter.2
  203.8 43.5 all-reduce.9
  250.2 42.9 all-reduce.11
  295.3 27.8 reduce-scatter.4
  329.4 120.9 all-reduce.13
